TPU v7x, 32 devices: a whole 2x2x4 slice. The times are simulated.
32 devices in a mesh: gz: 4 (over y, core), xy: 8 (over z, x).
Axes of the slice: x: 2, y: 2, z: 4, core: 2. Of those that a mesh axis runs over, the one named last changes fastest.
Arguments:
- right_side: float32 [12, 8, 16, 512], P(None, 'gz', 'xy'), may hold values from -24 to 24
- jac_diag: bfloat16 [12, 12, 8, 16, 512], P(None, None, 'gz', 'xy'), may hold values from -1.25 to 7.05
- jac_off: bfloat16 [6, 12, 12, 8, 16, 512], P(None, None, None, 'gz', 'xy'), may hold values from -0.59765625 to 0.59765625
- block_inv: bfloat16 [12, 12, 8, 16, 512], P(None, None, 'gz', 'xy'), may hold values from -0.125 to 0.405
- press_weight: bfloat16 [12, 8, 16, 512], P(None, 'gz', 'xy'), may hold values from 0.099609375 to 1
- press_diag: bfloat16 [8, 16, 512], P('gz', 'xy'), may hold values from 6.5 to 9
- press_off: bfloat16 [6, 8, 16, 512], P(None, 'gz', 'xy'), may hold values from -1 to -0.19921875
- well_index: float32 [8, 16, 512], P('gz', 'xy'), may hold values from 0.5 to 5
- well_columns: int32 [64], replicated, may hold values from 0 to 8191
- agg_map: int32 [8, 16, 512], P('gz', 'xy'), may hold values from 0 to 7
- level1_op: bfloat16 [8, 8, 8, 16, 4], P(None, None, 'gz', 'xy'), may hold values from -1.65 to 5.05
- coarsest_inv: bfloat16 [8, 16, 8, 16], P('gz', 'xy'), may hold values from -0.13479223 to 0.31156893
Outputs:
- solution: float32 [12, 8, 16, 512], P(None, 'gz', 'xy')
- residual: float32 [12, 8, 16, 512], P(None, 'gz', 'xy')
- hessenberg: float32 [3, 2], replicated
Inputs may be any that keep to these rules, and one draw needn't show every extreme that they name: `well_columns`: flat areal index x * 512 + y of each vertical well, which is perforated in every layer; a column may hold several wells. `agg_map`: an aggregate may be empty.
All inputs are finite; a program needn't handle non-finite values.
Results may differ from a plain program's by a relative error of at most 0.0018.
Values may be sent and summed in bfloat16 or wider, within the bound.
A program may use at most 64 MiB of HBM per device.

v0:
```python
import jax
import jax.numpy as jnp
from jax import lax
from jax.sharding import PartitionSpec as P

ITERS = 2


EPSILON = 1e-06


def padded_2(block, sides, width):
    for axis, dim in sides:
        count = lax.axis_size(axis)
        forward = [(i, i + 1) for i in range(count - 1)]
        backward = [(target, source) for source, target in forward]
        low = lax.ppermute(
            lax.slice_in_dim(block, block.shape[dim] - width, None, axis=dim), axis, forward
        )
        high = lax.ppermute(lax.slice_in_dim(block, 0, width, axis=dim), axis, backward)
        block = jnp.concatenate([low, block, high], axis=dim)
    return block


def neighbours(padded):
    return jnp.stack(
        [
            padded[..., :-2, 1:-1, 1:-1],
            padded[..., 2:, 1:-1, 1:-1],
            padded[..., 1:-1, :-2, 1:-1],
            padded[..., 1:-1, 2:, 1:-1],
            padded[..., 1:-1, 1:-1, :-2],
            padded[..., 1:-1, 1:-1, 2:],
        ]
    )


def pad_along_y(field):
    widths = [(0, 0)] * (field.ndim - 1) + [(1, 1)]
    return jnp.pad(field, widths)


def fine_near(field):
    padded = padded_2(field, (("gz", 1), ("xy", 2)), 1)
    return neighbours(pad_along_y(padded))


def pressure_near(field):
    padded = padded_2(field, (("gz", 0), ("xy", 1)), 1)
    return neighbours(pad_along_y(padded))


def least_squares(hessen, beta):
    upper = [list(line) for line in hessen]
    target = [beta] + [jnp.zeros((), jnp.float32) for line in range(ITERS)]
    rotations = []
    for column in range(ITERS):
        for row, (cosine, sine) in enumerate(rotations):
            first, second = (upper[row][column], upper[row + 1][column])
            upper[row][column] = cosine * first + sine * second
            upper[row + 1][column] = cosine * second - sine * first
        first, second = (upper[column][column], upper[column + 1][column])
        radius = jnp.sqrt(first * first + second * second)
        cosine, sine = (first / radius, second / radius)
        upper[column][column] = radius
        leading = target[column]
        target[column] = cosine * leading
        target[column + 1] = -sine * leading
        rotations.append((cosine, sine))
    weights = [None] * ITERS
    for column in reversed(range(ITERS)):
        total = target[column]
        for later in range(column + 1, ITERS):
            total = total - upper[column][later] * weights[later]
        weights[column] = total / upper[column][column]
    return weights


def on_device(
    right_side,
    jac_diag,
    jac_off,
    block_inv,
    press_weight,
    press_diag,
    press_off,
    well_index,
    well_columns,
    agg_map,
    level1_op,
    coarsest_inv,
):
    depth, width, length = (right_side.shape[1], right_side.shape[2], right_side.shape[3])
    aggregates = level1_op.shape[0]
    blocks = level1_op.shape[4]
    block_len = length // blocks
    layer_devices = lax.axis_size("gz")
    areal_devices = lax.axis_size("xy")
    columns = (
        lax.axis_index("xy") * width + jnp.arange(width, dtype=jnp.int32)[:, None]
    ) * length + jnp.arange(length, dtype=jnp.int32)[None, :]
    well_mask = (well_columns[:, None] == columns.reshape(1, -1)).astype(jnp.float32)
    wells_here = jnp.sum(well_mask, axis=0).reshape(width, length)
    local_weight = jnp.dot(
        well_mask, jnp.sum(well_index, axis=0).reshape(-1), precision=lax.Precision.HIGHEST
    )
    local_norm = jnp.sum(right_side * right_side)
    norm_squared, well_weight = lax.psum((local_norm, local_weight), ("gz", "xy"))

    def well_term(pressure):
        local = jnp.dot(
            well_mask,
            jnp.sum(well_index * pressure, axis=0).reshape(-1),
            precision=lax.Precision.HIGHEST,
        )
        totals = lax.psum(local, ("gz", "xy"))
        spread = jnp.dot(totals / well_weight, well_mask, precision=lax.Precision.HIGHEST).reshape(
            width, length
        )
        return well_index * (wells_here * pressure - spread)

    def apply_column(pressure):
        near = pressure_near(pressure)
        result = jac_diag[:, 0].astype(jnp.float32) * pressure[None]
        result = result + jnp.sum(jac_off[:, :, 0].astype(jnp.float32) * near[:, None], axis=0)
        return result.at[0].add(well_term(pressure))

    diag_pressure = press_diag.astype(jnp.float32)

    def apply_pressure(field):
        near = pressure_near(field)
        return diag_pressure * field + jnp.sum(press_off.astype(jnp.float32) * near, axis=0)

    one_hot = (
        agg_map[None] == jnp.arange(aggregates, dtype=jnp.int32)[:, None, None, None]
    ).astype(jnp.float32)
    coarse_op = level1_op.astype(jnp.float32)
    coarse_diag = jnp.stack([coarse_op[index, index] for index in range(aggregates)])
    beta = jnp.sqrt(norm_squared + EPSILON)
    basis = [right_side / beta]
    directions = []
    images = []
    hessen = [[jnp.zeros((), jnp.float32) for column in range(ITERS)] for row in range(ITERS + 1)]
    for step in range(ITERS):
        precondition_vector = basis[step]
        pressure_rhs = jnp.sum(press_weight.astype(jnp.float32) * precondition_vector, axis=0)
        first_guess = pressure_rhs / diag_pressure
        fine_rest = pressure_rhs - apply_pressure(first_guess)
        coarse_rhs = jnp.sum(
            (one_hot * fine_rest[None]).reshape(aggregates, depth, width, blocks, block_len),
            axis=-1,
        )
        coarse_guess = coarse_rhs / coarse_diag
        coarse_rest = coarse_rhs - jnp.sum(coarse_op * coarse_guess[None], axis=1)
        coarsest_rhs = jnp.sum(coarse_rest, axis=(0, 3)).astype(jnp.bfloat16)
        gathered = lax.all_gather(coarsest_rhs.reshape(-1), ("gz", "xy"), axis=0, tiled=True)
        ordered = (
            gathered.reshape(layer_devices, areal_devices, depth, width)
            .transpose(0, 2, 1, 3)
            .reshape(-1)
        )
        coarsest = jnp.dot(
            coarsest_inv.reshape(depth * width, -1), ordered, preferred_element_type=jnp.float32
        ).reshape(depth, width)
        coarse_value = coarse_guess + coarsest[None, :, :, None]
        smooth_guess = first_guess + jnp.sum(
            one_hot * jnp.repeat(coarse_value, block_len, axis=-1), axis=0
        )
        precondition_pressure = (
            smooth_guess + (pressure_rhs - apply_pressure(smooth_guess)) / diag_pressure
        )
        remainder = precondition_vector - apply_column(precondition_pressure)
        correction = jnp.sum(block_inv.astype(jnp.float32) * remainder[None], axis=1)
        direction = correction.at[0].add(precondition_pressure)
        apply_near = fine_near(direction)
        centre = jnp.sum(jac_diag.astype(jnp.float32) * direction[None], axis=1)
        coupled = jnp.sum(jac_off.astype(jnp.float32) * apply_near[:, None], axis=(0, 2))
        apply_result = centre + coupled
        image = apply_result.at[0].add(well_term(direction[0]))
        directions.append(direction)
        images.append(image)
        products = jnp.stack([jnp.sum(image * vector) for vector in basis])
        coeffs = lax.psum(products, ("gz", "xy"))
        rest = image
        for row in range(step + 1):
            rest = rest - coeffs[row] * basis[row]
        height = jnp.sqrt(lax.psum(jnp.sum(rest * rest), ("gz", "xy")) + EPSILON)
        for row in range(step + 1):
            hessen[row][step] = coeffs[row]
        hessen[step + 1][step] = height
        if step + 1 < ITERS:
            basis.append(rest / height)
    weights = least_squares(hessen, beta)
    solution = weights[0] * directions[0]
    step = 1
    solution = solution + weights[step] * directions[step]
    applied = weights[0] * images[0]
    step = 1
    applied = applied + weights[step] * images[step]
    residual = right_side - applied
    hessenberg = jnp.stack([jnp.stack(line) for line in hessen])
    return (solution, residual, hessenberg)


def solution(mesh):
    in_specs = (
        P(None, "gz", "xy", None),
        P(None, None, "gz", "xy", None),
        P(None, None, None, "gz", "xy", None),
        P(None, None, "gz", "xy", None),
        P(None, "gz", "xy", None),
        P("gz", "xy", None),
        P(None, "gz", "xy", None),
        P("gz", "xy", None),
        P(),
        P("gz", "xy", None),
        P(None, None, "gz", "xy", None),
        P("gz", "xy", None, None),
    )
    out_specs = (P(None, "gz", "xy", None), P(None, "gz", "xy", None), P())
    return jax.shard_map(
        on_device, mesh=mesh, in_specs=in_specs, out_specs=out_specs, check_vma=False
    )
```

profile of v0, /device:TPU:0, one launch (start us, length us, event | category | flops | bytes accessed | tf_op | source)
XLA Modules:
  0.0 670.0 jit_solution(4432218615825731091)
XLA Ops:
  2.3 42.2 %psum.70 = f32[]{:T(128)} all-reduce(f32[]{:T(128)} %multiply_reduce_fusion.5), channel_id=1, replica_groups=mesh['gz'=4,'xy'=8] {'gz','xy'}, use_global_device_ids=true, to_apply=%region_1.0 | all-reduce | flops 1 | bytes 8 | tf_op jit(solution)/shard_map/psum | solution.py:108
  57.8 4.6 collective-permute-done.3
  65.0 43.6 %all-reduce.8 = bf16[128]{0:T(256)(128)(2,1)S(1)} all-reduce(bf16[128]{0:T(256)(128)(2,1)S(1)} %dynamic-update-slice.18), channel_id=1, replica_groups=mesh['gz'=4,'xy'=8] {'gz','xy'}, use_global_device_ids=true, to_apply=%add.8 | all-reduce | flops 128 | bytes 512
  112.1 4.1 collective-permute-done.5
  119.6 4.2 collective-permute-done.7
  129.1 42.7 %all-reduce.10 = (f32[64]{0:T(128)S(1)}, f32[64]{0:T(128)S(1)}) all-reduce(f32[64]{0:T(128)S(1)} %convolution_bitcast_fusion.4, f32[64]{0:T(128)S(1)} %convolution_bitcast_fusion.3), channel_id=1, replica_groups=mesh['gz'=4,'xy'=8] {'gz','xy'}, use_global_device_ids=true, to_apply=%region_12.13 | all-reduce | flops 128 | bytes 1024 | tf_op jit(solution)/shard_map/psum | solution.py:116
  172.2 4.2 collective-permute-start.10
  177.7 4.2 collective-permute-done.11
  189.9 42.5 %psum.73 = f32[64]{0:T(128)S(1)} all-reduce(f32[64]{0:T(128)S(1)} %convolution_bitcast_fusion.2), channel_id=1, replica_groups=mesh['gz'=4,'xy'=8] {'gz','xy'}, use_global_device_ids=true, to_apply=%region_19.20 | all-reduce | flops 64 | bytes 512 | tf_op jit(solution)/shard_map/psum | solution.py:116
  238.3 4.2 collective-permute-start.14
  252.2 3.7 fusion
  257.5 40.2 %psum.74 = f32[1]{0:T(128)} all-reduce(f32[1]{0:T(128)} %bitcast.48), channel_id=1, replica_groups=mesh['gz'=4,'xy'=8] {'gz','xy'}, use_global_device_ids=true, to_apply=%region_21.22 | all-reduce | flops 1 | bytes 8 | tf_op jit(solution)/shard_map/psum | solution.py:183
  299.9 39.7 %psum.75 = f32[]{:T(128)} all-reduce(f32[]{:T(128)} %multiply_reduce_fusion.3), channel_id=1, replica_groups=mesh['gz'=4,'xy'=8] {'gz','xy'}, use_global_device_ids=true, to_apply=%region_23.24 | all-reduce | flops 1 | bytes 8 | tf_op jit(solution)/shard_map/psum | solution.py:187
  345.9 4.5 collective-permute-done.17
  350.4 3.8 collective-permute-start.18
  355.6 4.2 collective-permute-done.19
  372.4 40.7 %all-reduce.9 = bf16[128]{0:T(256)(128)(2,1)} all-reduce(bf16[128]{0:T(256)(128)(2,1)} %dynamic-update-slice.19), channel_id=1, replica_groups=mesh['gz'=4,'xy'=8] {'gz','xy'}, use_global_device_ids=true, to_apply=%add.9 | all-reduce | flops 128 | bytes 512
  431.7 4.2 collective-permute-done.23
  444.2 42.7 %psum.76 = f32[64]{0:T(128)} all-reduce(f32[64]{0:T(128)S(1)} %convolution_bitcast_fusion.1), channel_id=1, replica_groups=mesh['gz'=4,'xy'=8] {'gz','xy'}, use_global_device_ids=true, to_apply=%region_33.34 | all-reduce | flops 64 | bytes 512 | tf_op jit(solution)/shard_map/psum | solution.py:116
  490.5 4.2 collective-permute-start.26
  510.2 42.8 %psum.77 = f32[64]{0:T(128)} all-reduce(f32[64]{0:T(128)} %convolution_bitcast_fusion), channel_id=1, replica_groups=mesh['gz'=4,'xy'=8] {'gz','xy'}, use_global_device_ids=true, to_apply=%region_38.39 | all-reduce | flops 64 | bytes 512 | tf_op jit(solution)/shard_map/psum | solution.py:116
  559.4 4.2 collective-permute-start.30
  578.9 40.2 %psum.78 = f32[2]{0:T(128)S(1)} all-reduce(f32[2]{0:T(128)S(1)} %pad_maximum_fusion.73), channel_id=1, replica_groups=mesh['gz'=4,'xy'=8] {'gz','xy'}, use_global_device_ids=true, to_apply=%region_41.42 | all-reduce | flops 2 | bytes 16 | tf_op jit(solution)/shard_map/psum | solution.py:183
  625.0 39.6 %psum.79 = f32[]{:T(128)} all-reduce(f32[]{:T(128)} %multiply_reduce_fusion), channel_id=1, replica_groups=mesh['gz'=4,'xy'=8] {'gz','xy'}, use_global_device_ids=true, to_apply=%region_43.44 | all-reduce | flops 1 | bytes 8 | tf_op jit(solution)/shard_map/psum | solution.py:187
  (311 shorter events, 150.2 us)
Async XLA Ops:
  48.2 5.8 collective-permute-start.1
  56.5 6.0 collective-permute-start.3
  110.6 5.6 collective-permute-start.5
  118.2 5.5 collective-permute-start.7
  124.1 48.0 %collective-permute-start.8 = (f32[1,2,512]{2,1,0:T(2,128)S(1)}, f32[1,2,512]{2,1,0:T(2,128)S(1)}, u32[]{:S(2)}, u32[]{:S(2)}) collective-permute-start(f32[1,2,512]{2,1,0:T(2,128)S(1)} %get-tuple-element.135), channel_id=1, source_target_pairs={{0,8},{8,16},{16,24},{1,9},{9,17},{17,25},{2,10},{10,18},{18,26},{... | collective-permute-start | bytes 12296 | tf_op jit(solution)/shard_map/ppermute | solution.py:17
  127.3 44.9 %collective-permute-start.9 = (f32[1,2,512]{2,1,0:T(2,128)S(1)}, f32[1,2,512]{2,1,0:T(2,128)S(1)}, u32[]{:S(2)}, u32[]{:S(2)}) collective-permute-start(f32[1,2,512]{2,1,0:T(2,128)S(1)} %get-tuple-element.134), channel_id=1, source_target_pairs={{8,0},{16,8},{24,16},{9,1},{17,9},{25,17},{10,2},{18,10},{26,18},{... | collective-permute-start | bytes 12296 | tf_op jit(solution)/shard_map/ppermute | solution.py:20
  172.2 5.5 collective-permute-start.10
  176.4 5.5 collective-permute-start.11
  186.5 50.6 %collective-permute-start.12 = (f32[12,1,2,512]{3,2,1,0:T(2,128)}, f32[12,1,2,512]{3,2,1,0:T(2,128)}, u32[]{:S(2)}, u32[]{:S(2)}) collective-permute-start(f32[12,1,2,512]{3,2,1,0:T(2,128)} %get-tuple-element.107), channel_id=1, source_target_pairs={{0,8},{8,16},{16,24},{1,9},{9,17},{17,25},{2,10},{10,18},{18,26},{... | collective-permute-start | bytes 147464 | tf_op jit(solution)/shard_map/ppermute | solution.py:17
  188.4 48.7 %collective-permute-start.13 = (f32[12,1,2,512]{3,2,1,0:T(2,128)}, f32[12,1,2,512]{3,2,1,0:T(2,128)}, u32[]{:S(2)}, u32[]{:S(2)}) collective-permute-start(f32[12,1,2,512]{3,2,1,0:T(2,128)} %get-tuple-element.106), channel_id=1, source_target_pairs={{8,0},{16,8},{24,16},{9,1},{17,9},{25,17},{10,2},{18,10},{26,18},{... | collective-permute-start | bytes 147464 | tf_op jit(solution)/shard_map/ppermute | solution.py:20
  238.3 7.4 %collective-permute-start.14 = (f32[12,4,1,512]{3,2,1,0:T(1,128)S(1)}, f32[12,4,1,512]{3,2,1,0:T(1,128)S(1)}, u32[]{:S(2)}, u32[]{:S(2)}) collective-permute-start(f32[12,4,1,512]{3,2,1,0:T(1,128)S(1)} %get-tuple-element.103), channel_id=1, source_target_pairs={{0,1},{1,2},{2,3},{3,4},{4,5},{5,6},{6,7},{8,9},{9,10},{10,11},{11... | collective-permute-start | bytes 294920 | tf_op jit(solution)/shard_map/ppermute | solution.py:17
  242.5 6.5 collective-permute-start.15
  344.6 5.8 collective-permute-start.17
  354.2 5.5 collective-permute-start.19
  422.1 6.0 collective-permute-start.21
  430.4 5.5 collective-permute-start.23
  438.3 51.5 %collective-permute-start.24 = (f32[1,2,512]{2,1,0:T(2,128)}, f32[1,2,512]{2,1,0:T(2,128)}, u32[]{:S(2)}, u32[]{:S(2)}) collective-permute-start(f32[1,2,512]{2,1,0:T(2,128)} %get-tuple-element.129), channel_id=1, source_target_pairs={{0,8},{8,16},{16,24},{1,9},{9,17},{17,25},{2,10},{10,18},{18,26},{... | collective-permute-start | bytes 12296 | tf_op jit(solution)/shard_map/ppermute | solution.py:17
  442.0 47.8 %collective-permute-start.25 = (f32[1,2,512]{2,1,0:T(2,128)}, f32[1,2,512]{2,1,0:T(2,128)}, u32[]{:S(2)}, u32[]{:S(2)}) collective-permute-start(f32[1,2,512]{2,1,0:T(2,128)} %get-tuple-element.128), channel_id=1, source_target_pairs={{8,0},{16,8},{24,16},{9,1},{17,9},{25,17},{10,2},{18,10},{26,18},{... | collective-permute-start | bytes 12296 | tf_op jit(solution)/shard_map/ppermute | solution.py:20
  490.5 7.1 %collective-permute-start.26 = (f32[4,1,512]{2,1,0:T(1,128)S(1)}, f32[4,1,512]{2,1,0:T(1,128)S(1)}, u32[]{:S(2)}, u32[]{:S(2)}) collective-permute-start(f32[4,1,512]{2,1,0:T(1,128)S(1)} %get-tuple-element.117), channel_id=1, source_target_pairs={{0,1},{1,2},{2,3},{3,4},{4,5},{5,6},{6,7},{8,9},{9,10},{10,11},{11... | collective-permute-start | bytes 24584 | tf_op jit(solution)/shard_map/ppermute | solution.py:17
  494.7 5.5 collective-permute-start.27
  506.1 52.1 %collective-permute-start.28 = (f32[12,1,2,512]{3,2,1,0:T(2,128)}, f32[12,1,2,512]{3,2,1,0:T(2,128)}, u32[]{:S(2)}, u32[]{:S(2)}) collective-permute-start(f32[12,1,2,512]{3,2,1,0:T(2,128)} %get-tuple-element.105), channel_id=1, source_target_pairs={{0,8},{8,16},{16,24},{1,9},{9,17},{17,25},{2,10},{10,18},{18,26},{... | collective-permute-start | bytes 147464 | tf_op jit(solution)/shard_map/ppermute | solution.py:17
  508.0 50.2 %collective-permute-start.29 = (f32[12,1,2,512]{3,2,1,0:T(2,128)}, f32[12,1,2,512]{3,2,1,0:T(2,128)}, u32[]{:S(2)}, u32[]{:S(2)}) collective-permute-start(f32[12,1,2,512]{3,2,1,0:T(2,128)} %get-tuple-element.104), channel_id=1, source_target_pairs={{8,0},{16,8},{24,16},{9,1},{17,9},{25,17},{10,2},{18,10},{26,18},{... | collective-permute-start | bytes 147464 | tf_op jit(solution)/shard_map/ppermute | solution.py:20
  559.4 7.3 %collective-permute-start.30 = (f32[12,4,1,512]{3,2,1,0:T(1,128)S(1)}, f32[12,4,1,512]{3,2,1,0:T(1,128)S(1)}, u32[]{:S(2)}, u32[]{:S(2)}) collective-permute-start(f32[12,4,1,512]{3,2,1,0:T(1,128)S(1)} %get-tuple-element.101), channel_id=1, source_target_pairs={{0,1},{1,2},{2,3},{3,4},{4,5},{5,6},{6,7},{8,9},{9,10},{10,11},{11... | collective-permute-start | bytes 294920 | tf_op jit(solution)/shard_map/ppermute | solution.py:17
  563.6 6.5 collective-permute-start.31
  (43 other events, 1468.6 us)
where the time goes:
time: 675 us; the launch traced here: 670 us
  blocking collectives  457 us (68%)
  other arithmetic  66.5 us (10%)
  starting transfers between devices  63.9 us (9%)
  waiting for transfers between devices  42.8 us (6%)
  local copies, waits for them, and re-layouts  23.5 us (3%)
  between operations  8.61 us (1%)
  matrix products  7.61 us (1%)
    psum x4, blocking collectives, well_term(): totals = lax.psum(local, ('gz', 'xy'))  171 us
    unnamed x2, blocking collectives  84.4 us
    psum x2, blocking collectives, on_device(): coeffs = lax.psum(products, ('gz', 'xy'))  80.4 us
    psum x2, blocking collectives, on_device(): height = jnp.sqrt(lax.psum(jnp.sum(rest * rest), ('gz', 'xy')) + EPSILON)  79.3 us
    ppermute x16, starting transfers between devices, padded_2(): lax.ppermute(lax.slice_in_dim(block, block.shape[dim] - width, None, axis...  42.9 us
    ppermute x16, waiting for transfers between devices, padded_2(): lax.ppermute(lax.slice_in_dim(block, 0, width, axis=dim), axis, backward)  42.6 us
    psum x1, blocking collectives, on_device(): lax.psum((local_norm, local_weight), ('gz', 'xy'))  42.2 us
    ppermute x16, starting transfers between devices, padded_2(): lax.ppermute(lax.slice_in_dim(block, 0, width, axis=dim), axis, backward)  21 us
  transfers between devices with their start and end apart: 32, of which 12 were waited for; matrix products, arithmetic and copies ran while one was open for 4% of the time, Pallas kernels for 0%

commit v1 on v0

v1 whole, which is shorter than its diff:
```python
import functools

import jax
import jax.numpy as jnp
from jax import lax
from jax.experimental import pallas as pl
from jax.experimental.pallas import tpu as pltpu
from jax.sharding import PartitionSpec as P

ITERS = 2
EPSILON = 1e-06
LANES = 128
TINY = 1e-30
F32 = jnp.float32
MESH = pl.DeviceIdType.MESH
ROUNDS = 6


def kernel(
    depth, width, length, layer_devices, areal_devices, halves,
    rs, pw, pd, po, wi, wc, agg, lvl, inv, jd_hbm, jo_hbm, bi_hbm,
    sol, res, hess,
    jd, jo, bi, basis, dirs, imgs, near, rem, cvec,
    fld, pkx, hz, hx, pkx12, hz12, hx12,
    invs, invh, rows_src, gath, co_src, co_gath, col_src, peer,
    hbm_sem, halo_send, halo_recv, big_send, big_recv, inv_send, inv_recv,
    row_send, row_recv, co_send, co_recv, peer_send, peer_recv,
):
    comps = rs.shape[0]
    strips = length // LANES
    plane = strips * width
    total = depth * plane
    count = layer_devices * areal_devices
    points = depth * width
    co_rows = invs.shape[0] // points
    aggregates = halves
    g = lax.axis_index("gz")
    e = lax.axis_index("xy")
    me = g * areal_devices + e

    def at(index):
        return {"gz": index // areal_devices, "xy": index % areal_devices}

    barrier = pltpu.get_barrier_semaphore()

    def greet(step, carry):
        pl.semaphore_signal(
            barrier, inc=1, device_id=at((me + step) % count), device_id_type=MESH
        )
        return carry

    lax.fori_loop(1, count, greet, 0)

    loads = [
        pltpu.make_async_copy(jd_hbm, jd, hbm_sem.at[0]),
        pltpu.make_async_copy(bi_hbm, bi, hbm_sem.at[1]),
        pltpu.make_async_copy(jo_hbm, jo, hbm_sem.at[2]),
    ]
    for load in loads:
        load.start()

    row_at = lax.broadcasted_iota(jnp.int32, (plane, LANES), 0)
    lane_at = lax.broadcasted_iota(jnp.int32, (plane, LANES), 1)
    x_at = row_at % width
    strip_at = row_at // width
    lane_row = lax.broadcasted_iota(jnp.int32, (1, LANES), 1)

    def roll(a, shift, axis):
        size = a.shape[axis]
        shift = shift % size
        return a if shift == 0 else pltpu.roll(a, shift, axis)

    def planes(a):
        return a.reshape(-1, plane, LANES)

    def pack(a, edge):
        p = planes(a).reshape(-1, depth, plane, LANES)
        groups = -(-depth // width)
        out = []
        for group in range(groups):
            acc = jnp.zeros((p.shape[0], plane, LANES), F32)
            for s in range(group * width, min(depth, (group + 1) * width)):
                moved = roll(p[:, s], s % width - edge, 1)
                acc = jnp.where((x_at == s % width)[None], moved, acc)
            out.append(acc)
        return out[0] if groups == 1 else jnp.concatenate(out, axis=1)

    def unpack(b, target):
        parts = []
        for s in range(depth):
            group = s // width
            piece = b[:, group * plane:(group + 1) * plane]
            parts.append(roll(piece, target - s % width, 1))
        return jnp.concatenate(parts, axis=1)

    def tile_rows(mask):
        return jnp.concatenate([mask] * depth, axis=0)[None]

    x_all = tile_rows(x_at)
    def shift_zl(f, h):
        return jnp.concatenate([h, f[:, :-plane]], axis=1) if depth > 1 else h

    def shift_zh(f, h):
        return jnp.concatenate([f[:, plane:], h], axis=1) if depth > 1 else h

    def shift_xl(f, h):
        own = roll(planes(f), 1, 1).reshape(f.shape)
        return jnp.where(x_all == 0, h, own)

    def shift_xh(f, h):
        own = roll(planes(f), -1, 1).reshape(f.shape)
        return jnp.where(x_all == width - 1, h, own)

    def shift_yl(f):
        p = planes(f)
        t = roll(p, 1, 2)
        u = roll(t, width, 1)
        first = (lane_at == 0)[None]
        edge = (strip_at == 0)[None]
        return jnp.where(first, jnp.where(edge, 0.0, u), t).reshape(f.shape)

    def shift_yh(f):
        p = planes(f)
        t = roll(p, -1, 2)
        u = roll(t, -width, 1)
        last = (lane_at == LANES - 1)[None]
        edge = (strip_at == strips - 1)[None]
        return jnp.where(last, jnp.where(edge, 0.0, u), t).reshape(f.shape)

    to = [
        (g < layer_devices - 1, g > 0, {"gz": g + 1, "xy": e}),
        (g > 0, g < layer_devices - 1, {"gz": g - 1, "xy": e}),
        (e < areal_devices - 1, e > 0, {"gz": g, "xy": e + 1}),
        (e > 0, e < areal_devices - 1, {"gz": g, "xy": e - 1}),
    ]

    @pl.when(g == 0)
    def _():
        hz[:, 0] = jnp.zeros(hz.shape[:1] + hz.shape[2:], F32)
        hz12[:, 0] = jnp.zeros(hz12.shape[:1] + hz12.shape[2:], F32)
        invh[0] = jnp.zeros(invh.shape[1:], F32)

    @pl.when(g == layer_devices - 1)
    def _():
        hz[:, 1] = jnp.zeros(hz.shape[:1] + hz.shape[2:], F32)
        hz12[:, 1] = jnp.zeros(hz12.shape[:1] + hz12.shape[2:], F32)
        invh[1] = jnp.zeros(invh.shape[1:], F32)

    @pl.when(e == 0)
    def _():
        hx[:, 0] = jnp.zeros(hx.shape[:1] + hx.shape[2:], F32)
        hx12[:, 0] = jnp.zeros(hx12.shape[:1] + hx12.shape[2:], F32)
        invh[2] = jnp.zeros(invh.shape[1:], F32)

    @pl.when(e == areal_devices - 1)
    def _():
        hx[:, 1] = jnp.zeros(hx.shape[:1] + hx.shape[2:], F32)
        hx12[:, 1] = jnp.zeros(hx12.shape[:1] + hx12.shape[2:], F32)
        invh[3] = jnp.zeros(invh.shape[1:], F32)

    finals = []

    def halo_copies(r):
        srcs = [
            fld.at[r, pl.ds(total - plane, plane)],
            fld.at[r, pl.ds(0, plane)],
            pkx.at[r, 0],
            pkx.at[r, 1],
        ]
        dsts = [hz.at[r, 0], hz.at[r, 1], hx.at[r, 0], hx.at[r, 1]]
        return [
            pltpu.make_async_remote_copy(
                src_ref=srcs[d], dst_ref=dsts[d], send_sem=halo_send.at[r, d],
                recv_sem=halo_recv.at[r, d], device_id=to[d][2], device_id_type=MESH,
            )
            for d in range(4)
        ]

    def big_copies(t):
        srcs = [
            dirs.at[t, :, pl.ds(total - plane, plane)],
            dirs.at[t, :, pl.ds(0, plane)],
            pkx12.at[t, 0],
            pkx12.at[t, 1],
        ]
        dsts = [hz12.at[t, 0], hz12.at[t, 1], hx12.at[t, 0], hx12.at[t, 1]]
        return [
            pltpu.make_async_remote_copy(
                src_ref=srcs[d], dst_ref=dsts[d], send_sem=big_send.at[t, d],
                recv_sem=big_recv.at[t, d], device_id=to[d][2], device_id_type=MESH,
            )
            for d in range(4)
        ]

    def inv_copies():
        return [
            pltpu.make_async_remote_copy(
                src_ref=invs, dst_ref=invh.at[d], send_sem=inv_send.at[d],
                recv_sem=inv_recv.at[d], device_id=to[d][2], device_id_type=MESH,
            )
            for d in range(4)
        ]

    def start_all(copies):
        for d in range(4):
            pl.when(to[d][0])(copies[d].start)
            finals.append((to[d][0], copies[d].wait_send))

    def arrive(copies):
        for d in range(4):
            pl.when(to[d][1])(copies[d].wait_recv)

    def halo_start(r, f):
        fld[r] = f
        pkx[r, 0] = pack(f[None], width - 1)[0]
        pkx[r, 1] = pack(f[None], 0)[0]
        copies = halo_copies(r)
        start_all(copies)
        return copies

    def halo_read(r):
        return (
            hz[r, 0][None], hz[r, 1][None],
            unpack(hx[r, 0][None], 0), unpack(hx[r, 1][None], width - 1),
        )

    def send_all(src, dst, size, send, recv):
        def one(step, carry):
            pltpu.make_async_remote_copy(
                src_ref=src, dst_ref=dst.at[pl.ds(me * size, size)], send_sem=send,
                recv_sem=recv, device_id=at((me + step) % count), device_id_type=MESH,
            ).start()
            return carry

        lax.fori_loop(1, count, one, 0)
        whole = dst.at[pl.ds(0, (count - 1) * size)]
        finals.append((None, pltpu.make_async_copy(whole, whole, send).wait))
        return pltpu.make_async_copy(whole, whole, recv).wait

    def rows_start(r, values):
        row = jnp.zeros((1, LANES), F32)
        for q, value in enumerate(values):
            row = jnp.where(lane_row == q, value, row)
        rows_src[r] = row
        gath[r, pl.ds(me, 1)] = row
        return send_all(rows_src.at[r], gath.at[r], 1, row_send.at[r], row_recv.at[r])

    def rows_read(r, n):
        got = gath[r]
        lanes = lax.broadcasted_iota(jnp.int32, got.shape, 1)
        return [
            jnp.sum(jnp.where(lanes == q, got, 0.0), axis=1, keepdims=True) for q in range(n)
        ]

    def peers_start(r, value):
        col_src[r] = value
        peer[r, g] = value
        for step in range(1, layer_devices):
            pltpu.make_async_remote_copy(
                src_ref=col_src.at[r], dst_ref=peer.at[r, g], send_sem=peer_send.at[r],
                recv_sem=peer_recv.at[r],
                device_id={"gz": (g + step) % layer_devices, "xy": e}, device_id_type=MESH,
            ).start()
        whole = peer.at[r, pl.ds(0, layer_devices - 1)]
        finals.append((None, pltpu.make_async_copy(whole, whole, peer_send.at[r]).wait))
        return pltpu.make_async_copy(whole, whole, peer_recv.at[r]).wait

    def over_planes(f):
        acc = f[0:plane]
        for z in range(1, depth):
            acc = acc + f[z * plane:(z + 1) * plane]
        return acc

    def scalar(a):
        a = jnp.sum(a, axis=0) if a.ndim == 3 else a
        return jnp.sum(jnp.sum(a, axis=0, keepdims=True), axis=1, keepdims=True)

    def ssum(a):
        return jnp.sum(a, axis=0, keepdims=True)

    diag = pd[...].astype(F32)
    sides = po[...].astype(F32)
    rs_all = rs[...]
    raw_rhs = jnp.sum(pw[...].astype(F32) * rs_all, axis=0)
    raw_guess = raw_rhs / diag
    norm_here = scalar(rs_all * rs_all)
    index = wi[...]
    weight_here = over_planes(index)
    invs[...] = inv[...].astype(F32)
    column = (e * width + x_at) * length + strip_at * LANES + lane_at

    pl.semaphore_wait(barrier, count - 1)
    norm_wait = rows_start(0, [norm_here])
    halo_a = halo_start(0, raw_guess)
    inv_all = inv_copies()
    start_all(inv_all)
    weight_wait = peers_start(0, weight_here)

    def tally(w, acc):
        return acc + jnp.where(column == wc[w], 1.0, 0.0)

    wells = lax.fori_loop(0, wc.shape[0], tally, jnp.zeros((plane, LANES), F32))
    wells = jnp.concatenate([wells] * depth, axis=0)
    well_factor = index * wells
    aggs = agg[...]

    def apply_pressure(f, halos):
        f3 = f[None]
        nears = [
            shift_zl(f3, halos[0]), shift_zh(f3, halos[1]),
            shift_xl(f3, halos[2]), shift_xh(f3, halos[3]),
            shift_yl(f3), shift_yh(f3),
        ]
        out = diag * f
        for k in range(6):
            out = out + sides[k] * nears[k][0]
        return out

    def well_start(r, q):
        return peers_start(r, over_planes(index * q))

    norm_wait()
    beta = jnp.sqrt(ssum(rows_read(0, 1)[0]) + EPSILON)
    arrive(halo_a)
    guess_halos = [h / beta for h in halo_read(0)]
    arrive(inv_all)
    basis[0] = rs_all / beta
    rhs = raw_rhs / beta
    guess = raw_guess / beta

    col_weight = None
    hessen = [[jnp.zeros((1, 1), F32) for _ in range(ITERS)] for _ in range(ITERS + 1)]
    lane_all = lax.broadcasted_iota(jnp.int32, (total, LANES), 1)
    flat_at = (
        lax.broadcasted_iota(jnp.int32, (co_rows, LANES), 0) * LANES
        + lax.broadcasted_iota(jnp.int32, (co_rows, LANES), 1)
    )
    gram = None
    for t in range(ITERS):
        v = basis.at[t]
        rest = rhs - apply_pressure(guess, guess_halos)
        colsum = lvl[0]
        codiag = lvl[1]
        coarse = jnp.zeros((total, LANES), F32)
        for a in range(aggregates):
            part = jnp.sum(jnp.where(aggs == a, rest, 0.0), axis=1, keepdims=True)
            coarse = jnp.where(lane_all == a, part, coarse)
        coarse_guess = coarse / codiag
        coarse_rest = jnp.sum(coarse - colsum * coarse_guess, axis=1, keepdims=True)
        message = jnp.zeros((co_rows, LANES), F32)
        for z in range(depth):
            part = coarse_rest[z * plane:(z + 1) * plane]
            for x in range(width):
                value = jnp.sum(
                    jnp.where(x_at[:, 0:1] == x, part, 0.0), axis=0, keepdims=True
                )
                spot = (g * depth + z) * (areal_devices * width) + e * width + x
                message = jnp.where(flat_at == spot, value, message)
        message = message.astype(jnp.bfloat16).astype(F32)
        co_src[t] = message
        co_gath[t, pl.ds(me * co_rows, co_rows)] = message
        co_wait = send_all(co_src.at[t], co_gath.at[t], co_rows, co_send.at[t], co_recv.at[t])
        picked = guess
        for a in range(aggregates):
            picked = jnp.where(aggs == a, guess + coarse_guess[:, a:a + 1], picked)
        halo_b = halo_start(1 + 3 * t, picked)
        if t == 0:
            weight_wait()
            col_weight = jnp.sum(peer[0], axis=0)
        b0 = basis[0]
        if t == 0:
            g00 = scalar(b0 * b0)
        else:
            b1 = basis[1]
            g00, g01 = gram[0], scalar(b0 * b1)
            tilt = jnp.where(g00 > TINY, g01 / g00, 0.0)
            perp = b1 - tilt * b0
            cvec[...] = perp
            cc = scalar(perp * perp)
        gram = (g00,)
        co_wait()
        ordered = jnp.sum(co_gath[t].reshape(count, co_rows, LANES), axis=0)

        def coarsest_of(mat):
            prod = mat.reshape(points, co_rows, LANES) * ordered[None]
            return jnp.sum(jnp.sum(prod, axis=1), axis=1, keepdims=True)

        def layer_of(values, z):
            acc = jnp.zeros((plane, LANES), F32)
            for x in range(width):
                at_point = z * width + x
                acc = jnp.where(x_at == x, values[at_point:at_point + 1], acc)
            return acc

        def spread_of(values):
            return jnp.concatenate([layer_of(values, z) for z in range(depth)], axis=0)

        def edge_of(values, x):
            parts = [
                jnp.broadcast_to(
                    values[z * width + x:z * width + x + 1], (plane, LANES)
                )
                for z in range(depth)
            ]
            return jnp.concatenate(parts, axis=0)

        smooth = picked + spread_of(coarsest_of(invs[...]))
        halo_extra = [
            layer_of(coarsest_of(invh[0]), depth - 1),
            layer_of(coarsest_of(invh[1]), 0),
            edge_of(coarsest_of(invh[2]), width - 1),
            edge_of(coarsest_of(invh[3]), 0),
        ]
        arrive(halo_b)
        got = halo_read(1 + 3 * t)
        smooth_halos = [got[d] + halo_extra[d][None] for d in range(4)]
        pressure = smooth + (rhs - apply_pressure(smooth, smooth_halos)) / diag
        halo_d = halo_start(2 + 3 * t, pressure)
        well_wait = well_start(1 + 2 * t, pressure)
        if t == 0:
            for load in loads:
                load.wait()
        p3 = pressure[None]
        acc = v[...] - jd[:, 0].astype(F32) * p3
        acc = acc - jo[4, :, 0].astype(F32) * shift_yl(p3)
        acc = acc - jo[5, :, 0].astype(F32) * shift_yh(p3)
        arrive(halo_d)
        got = halo_read(2 + 3 * t)
        acc = acc - jo[0, :, 0].astype(F32) * shift_zl(p3, got[0])
        acc = acc - jo[1, :, 0].astype(F32) * shift_zh(p3, got[1])
        acc = acc - jo[2, :, 0].astype(F32) * shift_xl(p3, got[2])
        acc = acc - jo[3, :, 0].astype(F32) * shift_xh(p3, got[3])
        rem[...] = acc

        def well_term(r, q):
            level = jnp.sum(peer[r], axis=0) / col_weight
            return well_factor * (q - jnp.concatenate([level] * depth, axis=0))

        well_wait()
        rem[0] = rem[0] - well_term(1 + 2 * t, pressure)

        def correct(i, carry):
            dirs[t, i] = jnp.sum(bi[i].astype(F32) * rem[...], axis=0)
            return carry

        lax.fori_loop(0, comps, correct, 0)
        head = dirs[t, 0] + pressure
        dirs[t, 0] = head
        d_all = dirs[t]
        pkx12[t, 0] = pack(d_all, width - 1)
        pkx12[t, 1] = pack(d_all, 0)
        big = big_copies(t)
        start_all(big)
        well_wait = well_start(2 + 2 * t, head)
        near[4] = shift_yl(d_all)
        near[5] = shift_yh(d_all)

        def inner(i, carry):
            out = jnp.sum(jd[i].astype(F32) * dirs[t], axis=0)
            for k in (4, 5):
                out = out + jnp.sum(jo[k, i].astype(F32) * near[k], axis=0)
            imgs[t, i] = out
            return carry

        lax.fori_loop(0, comps, inner, 0)
        arrive(big)
        d_all = dirs[t]
        near[0] = shift_zl(d_all, hz12[t, 0])
        near[1] = shift_zh(d_all, hz12[t, 1])
        near[2] = shift_xl(d_all, unpack(hx12[t, 0], 0))
        near[3] = shift_xh(d_all, unpack(hx12[t, 1], width - 1))

        def outer(i, carry):
            out = imgs[t, i]
            for k in range(4):
                out = out + jnp.sum(jo[k, i].astype(F32) * near[k], axis=0)
            imgs[t, i] = out
            return carry

        lax.fori_loop(0, comps, outer, 0)
        well_wait()
        imgs[t, 0] = imgs[t, 0] + well_term(2 + 2 * t, head)
        image = imgs[t]
        b0 = basis[0]
        p0 = scalar(image * b0)
        a0 = jnp.where(g00 > TINY, p0 / g00, 0.0)
        if t == 0:
            left = image - a0 * b0
            rr = scalar(left * left)
            row_wait = rows_start(1, [p0, g00, a0, rr])
            image_guess = jnp.sum(pw[...].astype(F32) * image, axis=0) / diag
            halo_f = halo_start(3, image_guess)
            row_wait()
            q0, gg, aa, ll = rows_read(1, 4)
            h00 = ssum(q0)
            height = jnp.sqrt(ssum(ll + (aa - h00) * (aa - h00) * gg) + EPSILON)
            hessen[0][0] = h00
            hessen[1][0] = height
            next_basis = (image - h00 * b0) / height
            basis[1] = next_basis
            rhs = jnp.sum(pw[...].astype(F32) * next_basis, axis=0)
            guess = rhs / diag
            arrive(halo_f)
            got = halo_read(3)
            guess_halos = [(got[d] - h00 * guess_halos[d]) / height for d in range(4)]
        else:
            perp = cvec[...]
            p1 = scalar(image * basis[1])
            a1 = jnp.where(cc > TINY, scalar(image * perp) / cc, 0.0)
            left = image - a0 * b0 - a1 * perp
            rr = scalar(left * left)
            row_wait = rows_start(2, [p0, p1, g00, tilt, a0, cc, a1, rr])
            row_wait()
            q0, q1, gg, ee, aa0, cc1, aa1, ll = rows_read(2, 8)
            h0 = ssum(q0)
            h1 = ssum(q1)
            d0 = aa0 - h0 - ee * h1
            d1 = aa1 - h1
            hessen[0][1] = h0
            hessen[1][1] = h1
            hessen[2][1] = jnp.sqrt(ssum(ll + d0 * d0 * gg + d1 * d1 * cc1) + EPSILON)

    weights = least_squares(hessen, beta)
    sol[...] = weights[0] * dirs[0] + weights[1] * dirs[1]
    res[...] = rs[...] - (weights[0] * imgs[0] + weights[1] * imgs[1])
    hr = lax.broadcasted_iota(jnp.int32, hess.shape, 0)
    hc = lax.broadcasted_iota(jnp.int32, hess.shape, 1)
    table = jnp.zeros(hess.shape, F32)
    for i in range(ITERS + 1):
        for j in range(ITERS):
            table = jnp.where((hr == i) & (hc == j), hessen[i][j], table)
    hess[...] = table
    for condition, wait in finals:
        if condition is None:
            wait()
        else:
            pl.when(condition)(wait)


def least_squares(hessen, beta):
    upper = [list(line) for line in hessen]
    target = [beta] + [jnp.zeros((1, 1), F32) for line in range(ITERS)]
    rotations = []
    for column in range(ITERS):
        for row, (cosine, sine) in enumerate(rotations):
            first, second = (upper[row][column], upper[row + 1][column])
            upper[row][column] = cosine * first + sine * second
            upper[row + 1][column] = cosine * second - sine * first
        first, second = (upper[column][column], upper[column + 1][column])
        radius = jnp.sqrt(first * first + second * second)
        cosine, sine = (first / radius, second / radius)
        upper[column][column] = radius
        leading = target[column]
        target[column] = cosine * leading
        target[column + 1] = -sine * leading
        rotations.append((cosine, sine))
    weights = [None] * ITERS
    for column in reversed(range(ITERS)):
        total = target[column]
        for later in range(column + 1, ITERS):
            total = total - upper[column][later] * weights[later]
        weights[column] = total / upper[column][column]
    return weights


def to_rows(a):
    depth, width, length = a.shape[-3:]
    lead = a.shape[:-3]
    strips = length // LANES
    a = a.reshape(lead + (depth, width, strips, LANES))
    return jnp.swapaxes(a, -3, -2).reshape(lead + (depth * strips * width, LANES))


def from_rows(a, depth, width, length):
    lead = a.shape[:-2]
    strips = length // LANES
    a = a.reshape(lead + (depth, strips, width, LANES))
    return jnp.swapaxes(a, -3, -2).reshape(lead + (depth, width, length))


def on_device(
    right_side, jac_diag, jac_off, block_inv, press_weight, press_diag, press_off,
    well_index, well_columns, agg_map, level1_op, coarsest_inv,
):
    comps, depth, width, length = right_side.shape
    aggregates = level1_op.shape[0]
    blocks = level1_op.shape[4]
    layer_devices = lax.axis_size("gz")
    areal_devices = lax.axis_size("xy")
    count = layer_devices * areal_devices
    plane = (length // LANES) * width
    total = depth * plane
    points = depth * width
    op = level1_op.astype(F32)
    colsum = jnp.sum(op, axis=0)
    codiag = jnp.stack([op[a, a] for a in range(aggregates)])
    lane_pad = ((0, 0), (0, LANES - aggregates))
    order = (1, 3, 2, 0)
    colsum = colsum.transpose(order).reshape(total, aggregates)
    codiag = codiag.transpose(order).reshape(total, aggregates)
    lvl = jnp.stack(
        [jnp.pad(colsum, lane_pad), jnp.pad(codiag, lane_pad, constant_values=1.0)]
    )
    flat = coarsest_inv.shape[2] * coarsest_inv.shape[3]
    co_rows = flat // LANES
    inv = coarsest_inv.reshape(points * co_rows, LANES)

    vm = pl.BlockSpec(memory_space=pltpu.VMEM)
    sm = pl.BlockSpec(memory_space=pltpu.SMEM)
    anyspace = pl.BlockSpec(memory_space=pl.ANY)
    edge_rows = -(-depth // width) * plane
    v = pltpu.VMEM
    dma = pltpu.SemaphoreType.DMA
    scratch = [
        v((comps, comps, total, LANES), jnp.bfloat16),
        v((6, comps, comps, total, LANES), jnp.bfloat16),
        v((comps, comps, total, LANES), jnp.bfloat16),
        v((ITERS, comps, total, LANES), F32),
        v((ITERS, comps, total, LANES), F32),
        v((ITERS, comps, total, LANES), F32),
        v((6, comps, total, LANES), F32),
        v((comps, total, LANES), F32),
        v((comps, total, LANES), F32),
        v((ROUNDS, total, LANES), F32),
        v((ROUNDS, 2, edge_rows, LANES), F32),
        v((ROUNDS, 2, plane, LANES), F32),
        v((ROUNDS, 2, edge_rows, LANES), F32),
        v((ITERS, 2, comps, edge_rows, LANES), F32),
        v((ITERS, 2, comps, plane, LANES), F32),
        v((ITERS, 2, comps, edge_rows, LANES), F32),
        v((points * co_rows, LANES), F32),
        v((4, points * co_rows, LANES), F32),
        v((3, 1, LANES), F32),
        v((3, count, LANES), F32),
        v((ITERS, co_rows, LANES), F32),
        v((ITERS, count * co_rows, LANES), F32),
        v((5, plane, LANES), F32),
        v((5, layer_devices, plane, LANES), F32),
        dma((3,)),
        dma((ROUNDS, 4)), dma((ROUNDS, 4)),
        dma((ITERS, 4)), dma((ITERS, 4)),
        dma((4,)), dma((4,)),
        dma((3,)), dma((3,)),
        dma((ITERS,)), dma((ITERS,)),
        dma((5,)), dma((5,)),
    ]
    body = functools.partial(
        kernel, depth, width, length, layer_devices, areal_devices, aggregates
    )
    sol, res, hess = pl.pallas_call(
        body,
        out_shape=(
            jax.ShapeDtypeStruct((comps, total, LANES), F32),
            jax.ShapeDtypeStruct((comps, total, LANES), F32),
            jax.ShapeDtypeStruct((ITERS + 1, ITERS), F32),
        ),
        in_specs=[vm, vm, vm, vm, vm, sm, vm, vm, vm, anyspace, anyspace, anyspace],
        out_specs=(vm, vm, vm),
        scratch_shapes=scratch,
        compiler_params=pltpu.CompilerParams(
            collective_id=0, has_side_effects=True, vmem_limit_bytes=40 * 1024 * 1024
        ),
    )(
        to_rows(right_side), to_rows(press_weight), to_rows(press_diag), to_rows(press_off),
        to_rows(well_index), well_columns, to_rows(agg_map), lvl, inv,
        to_rows(jac_diag), to_rows(jac_off), to_rows(block_inv),
    )
    return (
        from_rows(sol, depth, width, length),
        from_rows(res, depth, width, length),
        hess,
    )


def solution(mesh):
    in_specs = (
        P(None, "gz", "xy", None),
        P(None, None, "gz", "xy", None),
        P(None, None, None, "gz", "xy", None),
        P(None, None, "gz", "xy", None),
        P(None, "gz", "xy", None),
        P("gz", "xy", None),
        P(None, "gz", "xy", None),
        P("gz", "xy", None),
        P(),
        P("gz", "xy", None),
        P(None, None, "gz", "xy", None),
        P("gz", "xy", None, None),
    )
    out_specs = (P(None, "gz", "xy", None), P(None, "gz", "xy", None), P())
    return jax.shard_map(
        on_device, mesh=mesh, in_specs=in_specs, out_specs=out_specs, check_vma=False
    )
```

time: 675 us -> 62.7 us (0.09)
  blocking collectives: 457 us -> 0 us
  other arithmetic: 66.5 us -> 1.56 us
  starting transfers between devices: 63.9 us -> 0 us
  Pallas kernels: 0 us -> 47.3 us
  waiting for transfers between devices: 42.8 us -> 0 us
  local copies, waits for them, and re-layouts: 23.5 us -> 12.4 us
  between operations: 8.61 us -> 0.69 us
  matrix products: 7.61 us -> 0 us
    psum x9 -> x0, blocking collectives: 373 us -> none  [the longest x4 171 us: well_term(): totals = lax.psum(local, ('gz', 'xy'))]
    unnamed x2 -> x0, blocking collectives: 84.4 us -> none
    ppermute x32 -> x0, starting transfers between devices: 63.9 us -> none  [the longest x16 42.9 us: padded_2(): lax.ppermute(lax.slice_in_dim(block, block.shape[dim] - width, None, axis...]
    pallas_call x0 -> x1, Pallas kernels: none -> 47.3 us  [on_device(): pl.pallas_call(body, out_shape=(jax.ShapeDtypeStruct((comps, total, LANES...]
    ppermute x32 -> x0, waiting for transfers between devices: 42.8 us -> none  [the longest x16 42.6 us: padded_2(): lax.ppermute(lax.slice_in_dim(block, 0, width, axis=dim), axis, backward)]
    reduce_sum x32 -> x1, other arithmetic: 35.1 us -> 0.79 us  [on_device(): colsum = jnp.sum(op, axis=0)]
    concatenate x16 -> x0, other arithmetic: 7.97 us -> none  [padded_2(): block = jnp.concatenate([low, block, high], axis=dim)]
    dot_general x11 -> x0, matrix products: 7.61 us -> none  [the longest x4 4.22 us: well_term(): jnp.dot(totals / well_weight, well_mask, precision=lax.Precision.HIGHEST)]
  transfers between devices with their start and end apart: 32 -> 0, of which waited for: 12 -> 0; matrix products, arithmetic and copies ran while one was open for 4% -> 0% of each run, Pallas kernels for 0% -> 0%
where the time goes in v1:
time: 62.7 us; the launch traced here: 62 us
  Pallas kernels  47.3 us (75%)
  local copies, waits for them, and re-layouts  12.4 us (20%)
  other arithmetic  1.56 us (2%)
  between operations  0.69 us (1%)
    pallas_call x1, Pallas kernels, on_device(): pl.pallas_call(body, out_shape=(jax.ShapeDtypeStruct((comps, total, LANES...  47.3 us
    unnamed x30, local copies, waits for them, and re-layouts  11.3 us

profile of v1, /device:TPU:0, one launch (start us, length us, event | category | flops | bytes accessed | tf_op | source)
XLA Modules:
  0.0 62.0 jit_solution(4624234564892479524)
XLA Ops:
  0.6 0.8 %reshape.95.inv = bf16[4,128]{1,0:T(4,128)(2,1)S(1)} reshape(bf16[2,2,8,16]{3,2,1,0:T(8,128)(2,1)} %param.23) | data formatting | bytes 2048 | tf_op jit(solution)/shard_map/reshape | solution.py:606
  1.4 0.8 %convert_reduce_fusion = f32[8,2,2,4]{0,3,2,1:T(4,128)S(1)} fusion(bf16[8,8,2,2,4]{1,4,3,2,0:T(4,128)(2,1)} %param.22), kind=kLoop, calls=%fused_computation.9 | loop fusion | flops 1920 | bytes 2560 | tf_op jit(solution)/shard_map/reduce_sum | solution.py:595
  2.2 0.8 %convert_element_type.5 = f32[8,8,2,2,4]{1,4,3,2,0:T(4,128)S(1)} convert(bf16[8,8,2,2,4]{1,4,3,2,0:T(4,128)(2,1)} %param.22) | non-fusion elementwise | flops 1024 | bytes 6144 | tf_op jit(solution)/shard_map/convert_element_type | solution.py:594
  3.0 0.2 slice_reduce_fusion
  3.3 0.1 copy.48
  3.4 0.0 copy-start
  3.4 2.0 %copy-done = bf16[6,12,12,2,2,512]{5,4,3,2,1,0:T(2,128)(2,1)S(1)} copy-done((bf16[6,12,12,2,2,512]{5,4,3,2,1,0:T(2,128)(2,1)S(1)}, bf16[6,12,12,2,2,512]{5,4,3,2,1,0:T(2,128)(2,1)}, u32[]{:S(2)}) %copy-start) | copy-done | bytes 3538968
  5.4 0.0 copy-start.1
  5.4 1.1 %copy-done.1 = bf16[12,12,2,2,512]{4,3,2,1,0:T(2,128)(2,1)S(1)} copy-done((bf16[12,12,2,2,512]{4,3,2,1,0:T(2,128)(2,1)S(1)}, bf16[12,12,2,2,512]{4,3,2,1,0:T(2,128)(2,1)}, u32[]{:S(2)}) %copy-start.1) | copy-done | bytes 589848
  6.5 0.0 copy-start.2
  6.5 1.1 %copy-done.2 = bf16[12,12,2,2,512]{4,3,2,1,0:T(2,128)(2,1)S(1)} copy-done((bf16[12,12,2,2,512]{4,3,2,1,0:T(2,128)(2,1)S(1)}, bf16[12,12,2,2,512]{4,3,2,1,0:T(2,128)(2,1)}, u32[]{:S(2)}) %copy-start.2) | copy-done | bytes 589848
  7.5 0.0 copy-start.3
  7.5 0.9 %copy-done.3 = f32[12,2,2,512]{3,2,1,0:T(2,128)S(1)} copy-done((f32[12,2,2,512]{3,2,1,0:T(2,128)S(1)}, f32[12,2,2,512]{3,2,1,0:T(2,128)}, u32[]{:S(2)}) %copy-start.3) | copy-done | bytes 98328
  8.4 0.0 copy-start.4
  8.4 0.8 %copy-done.4 = bf16[12,2,2,512]{3,2,1,0:T(2,128)(2,1)S(1)} copy-done((bf16[12,2,2,512]{3,2,1,0:T(2,128)(2,1)S(1)}, bf16[12,2,2,512]{3,2,1,0:T(2,128)(2,1)}, u32[]{:S(2)}) %copy-start.4) | copy-done | bytes 49176
  9.2 0.7 %copy-done.5 = bf16[6,2,2,512]{3,2,1,0:T(2,128)(2,1)S(1)} copy-done((bf16[6,2,2,512]{3,2,1,0:T(2,128)(2,1)S(1)}, bf16[6,2,2,512]{3,2,1,0:T(2,128)(2,1)}, u32[]{:S(2)}) %copy-start.5) | copy-done | bytes 24600
  10.0 0.7 %copy-done.6 = f32[2,2,512]{2,1,0:T(2,128)S(1)} copy-done((f32[2,2,512]{2,1,0:T(2,128)S(1)}, f32[2,2,512]{2,1,0:T(2,128)}, u32[]{:S(2)}) %copy-start.6) | copy-done | bytes 8216
  10.7 0.7 %copy-done.7 = s32[2,2,512]{2,1,0:T(2,128)S(1)} copy-done((s32[2,2,512]{2,1,0:T(2,128)S(1)}, s32[2,2,512]{2,1,0:T(2,128)}, u32[]{:S(2)}) %copy-start.7) | copy-done | bytes 8216
  11.4 0.7 %copy-done.8 = bf16[2,2,512]{2,1,0:T(2,128)(2,1)S(1)} copy-done((bf16[2,2,512]{2,1,0:T(2,128)(2,1)S(1)}, bf16[2,2,512]{2,1,0:T(2,128)(2,1)}, u32[]{:S(2)}) %copy-start.8) | copy-done | bytes 4120
  12.1 0.7 %copy-done.9 = s32[64]{0:T(128)S(1)} copy-done((s32[64]{0:T(128)S(1)}, s32[64]{0:T(128)}, u32[]{:S(2)}) %copy-start.9) | copy-done | bytes 280
  12.7 47.3 %shard_map.139 = (f32[12,16,128]{2,1,0:T(8,128)S(1)}, f32[12,16,128]{2,1,0:T(8,128)S(1)}, f32[3,2]{1,0:T(4,128)S(1)}) custom-call(f32[12,16,128]{2,1,0:T(8,128)S(1)} %bitcast.86, bf16[12,16,128]{2,1,0:T(8,128)(2,1)S(1)} %bitcast.87, bf16[16,128]{1,0:T(8,128)(2,1)S(1)} %bitcast.91, bf16[6,16,128]{2,1,0:T(8,128)(2,1)S(1)} %bitcast.88, f32[16,128]{1,0:T(8,128)S(1)} %bitcast.89, ...), custom_call_target="tpu_custom_call" | custom-call | tf_op jit(solution)/shard_map/pallas_call | solution.py:650
  60.0 0.6 %copy.54 = f32[3,2]{0,1:T(2,128)} copy(f32[3,2]{1,0:T(4,128)S(1)} %get-tuple-element.17) | data formatting | bytes 48
  60.7 0.6 %copy.64 = f32[12,2,2,512]{3,2,1,0:T(2,128)} copy(f32[12,2,2,512]{3,2,1,0:T(2,128)S(1)} %bitcast.85) | data formatting | bytes 196608
  61.3 0.6 %copy.65 = f32[12,2,2,512]{3,2,1,0:T(2,128)} copy(f32[12,2,2,512]{3,2,1,0:T(2,128)S(1)} %bitcast.84) | data formatting | bytes 196608
  (16 shorter events, 0.1 us)
Async XLA Ops:
  3.4 2.0 %copy-start = (bf16[6,12,12,2,2,512]{5,4,3,2,1,0:T(2,128)(2,1)S(1)}, bf16[6,12,12,2,2,512]{5,4,3,2,1,0:T(2,128)(2,1)}, u32[]{:S(2)}) copy-start(bf16[6,12,12,2,2,512]{5,4,3,2,1,0:T(2,128)(2,1)} %param.14) | copy-start | bytes 10616836
  5.4 1.1 %copy-start.1 = (bf16[12,12,2,2,512]{4,3,2,1,0:T(2,128)(2,1)S(1)}, bf16[12,12,2,2,512]{4,3,2,1,0:T(2,128)(2,1)}, u32[]{:S(2)}) copy-start(bf16[12,12,2,2,512]{4,3,2,1,0:T(2,128)(2,1)} %param.13) | copy-start | bytes 1769476
  6.5 1.1 %copy-start.2 = (bf16[12,12,2,2,512]{4,3,2,1,0:T(2,128)(2,1)S(1)}, bf16[12,12,2,2,512]{4,3,2,1,0:T(2,128)(2,1)}, u32[]{:S(2)}) copy-start(bf16[12,12,2,2,512]{4,3,2,1,0:T(2,128)(2,1)} %param.15) | copy-start | bytes 1769476
  7.5 0.9 %copy-start.3 = (f32[12,2,2,512]{3,2,1,0:T(2,128)S(1)}, f32[12,2,2,512]{3,2,1,0:T(2,128)}, u32[]{:S(2)}) copy-start(f32[12,2,2,512]{3,2,1,0:T(2,128)} %param.12) | copy-start | bytes 294916
  8.4 0.8 %copy-start.4 = (bf16[12,2,2,512]{3,2,1,0:T(2,128)(2,1)S(1)}, bf16[12,2,2,512]{3,2,1,0:T(2,128)(2,1)}, u32[]{:S(2)}) copy-start(bf16[12,2,2,512]{3,2,1,0:T(2,128)(2,1)} %param.16) | copy-start | bytes 147460
  9.2 0.7 %copy-start.5 = (bf16[6,2,2,512]{3,2,1,0:T(2,128)(2,1)S(1)}, bf16[6,2,2,512]{3,2,1,0:T(2,128)(2,1)}, u32[]{:S(2)}) copy-start(bf16[6,2,2,512]{3,2,1,0:T(2,128)(2,1)} %param.18) | copy-start | bytes 73732
  10.0 0.7 %copy-start.6 = (f32[2,2,512]{2,1,0:T(2,128)S(1)}, f32[2,2,512]{2,1,0:T(2,128)}, u32[]{:S(2)}) copy-start(f32[2,2,512]{2,1,0:T(2,128)} %param.19) | copy-start | bytes 24580
  10.7 0.7 %copy-start.7 = (s32[2,2,512]{2,1,0:T(2,128)S(1)}, s32[2,2,512]{2,1,0:T(2,128)}, u32[]{:S(2)}) copy-start(s32[2,2,512]{2,1,0:T(2,128)} %param.21) | copy-start | bytes 24580
  11.4 0.7 %copy-start.8 = (bf16[2,2,512]{2,1,0:T(2,128)(2,1)S(1)}, bf16[2,2,512]{2,1,0:T(2,128)(2,1)}, u32[]{:S(2)}) copy-start(bf16[2,2,512]{2,1,0:T(2,128)(2,1)} %param.17) | copy-start | bytes 12292
  12.1 0.7 %copy-start.9 = (s32[64]{0:T(128)S(1)}, s32[64]{0:T(128)}, u32[]{:S(2)}) copy-start(s32[64]{0:T(128)} %wc.1) | copy-start | bytes 772

commit v2 on v1

--- a/solution.py
+++ b/solution.py
@@ -18,8 +18,10 @@
 
 def kernel(
     depth, width, length, layer_devices, areal_devices, halves,
-    rs, pw, pd, po, wi, wc, agg, lvl, inv, jd_hbm, jo_hbm, bi_hbm,
+    rs_hbm, pw_hbm, pd_hbm, po_hbm, wi_hbm, wc_hbm, agg_hbm, lvl_hbm, inv_hbm,
+    jd_hbm, jo_hbm, bi_hbm,
     sol, res, hess,
+    rs, pw, pd, po, wi, wc, agg, lvl, inv,
     jd, jo, bi, basis, dirs, imgs, near, rem, cvec,
     fld, pkx, hz, hx, pkx12, hz12, hx12,
     invs, invh, rows_src, gath, co_src, co_gath, col_src, peer,
@@ -41,6 +43,17 @@
     def at(index):
         return {"gz": index // areal_devices, "xy": index % areal_devices}
 
+    pairs = [
+        (rs_hbm, rs), (pw_hbm, pw), (pd_hbm, pd), (wi_hbm, wi), (po_hbm, po),
+        (lvl_hbm, lvl), (inv_hbm, inv), (agg_hbm, agg), (wc_hbm, wc),
+        (jd_hbm, jd), (jo_hbm, jo), (bi_hbm, bi),
+    ]
+    loads = [
+        pltpu.make_async_copy(src, dst, hbm_sem.at[n]) for n, (src, dst) in enumerate(pairs)
+    ]
+    for load in loads:
+        load.start()
+
     barrier = pltpu.get_barrier_semaphore()
 
     def greet(step, carry):
@@ -51,13 +64,6 @@
 
     lax.fori_loop(1, count, greet, 0)
 
-    loads = [
-        pltpu.make_async_copy(jd_hbm, jd, hbm_sem.at[0]),
-        pltpu.make_async_copy(bi_hbm, bi, hbm_sem.at[1]),
-        pltpu.make_async_copy(jo_hbm, jo, hbm_sem.at[2]),
-    ]
-    for load in loads:
-        load.start()
 
     row_at = lax.broadcasted_iota(jnp.int32, (plane, LANES), 0)
     lane_at = lax.broadcasted_iota(jnp.int32, (plane, LANES), 1)
@@ -278,6 +284,8 @@
     def ssum(a):
         return jnp.sum(a, axis=0, keepdims=True)
 
+    for load in loads[:5]:
+        load.wait()
     diag = pd[...].astype(F32)
     sides = po[...].astype(F32)
     rs_all = rs[...]
@@ -286,7 +294,38 @@
     norm_here = scalar(rs_all * rs_all)
     index = wi[...]
     weight_here = over_planes(index)
-    invs[...] = inv[...].astype(F32)
+    for load in loads[5:9]:
+        load.wait()
+    nz, nx = inv.shape[2:]
+    per = LANES // nx
+    inv_z = lax.broadcasted_iota(jnp.int32, (nz, LANES), 0)
+    inv_lane = lax.broadcasted_iota(jnp.int32, (nz, LANES), 1)
+    for z in range(depth):
+        for x in range(width):
+            wide = jnp.concatenate([inv[z, x].astype(F32)] * per, axis=1)
+            wide = jnp.where(inv_lane // nx == inv_z % per, wide, 0.0)
+            point = z * width + x
+            for r in range(co_rows):
+                invs[pl.ds(point * co_rows + r, 1)] = jnp.sum(
+                    wide[r * per:(r + 1) * per], axis=0, keepdims=True
+                )
+    op = lvl[...].astype(F32)
+    op_sum = jnp.sum(op, axis=0)
+    op_lane = lax.broadcasted_iota(jnp.int32, op.shape[1:], len(op.shape) - 2)
+    op_diag = jnp.zeros(op.shape[1:], F32)
+    for a in range(aggregates):
+        op_diag = jnp.where(op_lane == a, op[a], op_diag)
+    op_row = lax.broadcasted_iota(jnp.int32, (plane, aggregates), 0)
+    parts = ([], [])
+    for z in range(depth):
+        for part, table in zip(parts, (op_sum, op_diag)):
+            acc = jnp.zeros((plane, aggregates), F32)
+            for x in range(width):
+                for b in range(strips):
+                    acc = jnp.where(op_row == b * width + x, table[z, x, b:b + 1], acc)
+            part.append(acc)
+    colsum = jnp.concatenate(parts[0], axis=0)
+    codiag = jnp.concatenate(parts[1], axis=0)
     column = (e * width + x_at) * length + strip_at * LANES + lane_at
 
     pl.semaphore_wait(barrier, count - 1)
@@ -330,7 +369,7 @@
 
     col_weight = None
     hessen = [[jnp.zeros((1, 1), F32) for _ in range(ITERS)] for _ in range(ITERS + 1)]
-    lane_all = lax.broadcasted_iota(jnp.int32, (total, LANES), 1)
+    lane_all = lax.broadcasted_iota(jnp.int32, (total, aggregates), 1)
     flat_at = (
         lax.broadcasted_iota(jnp.int32, (co_rows, LANES), 0) * LANES
         + lax.broadcasted_iota(jnp.int32, (co_rows, LANES), 1)
@@ -339,9 +378,7 @@
     for t in range(ITERS):
         v = basis.at[t]
         rest = rhs - apply_pressure(guess, guess_halos)
-        colsum = lvl[0]
-        codiag = lvl[1]
-        coarse = jnp.zeros((total, LANES), F32)
+        coarse = jnp.zeros((total, aggregates), F32)
         for a in range(aggregates):
             part = jnp.sum(jnp.where(aggs == a, rest, 0.0), axis=1, keepdims=True)
             coarse = jnp.where(lane_all == a, part, coarse)
@@ -418,7 +455,7 @@
         halo_d = halo_start(2 + 3 * t, pressure)
         well_wait = well_start(1 + 2 * t, pressure)
         if t == 0:
-            for load in loads:
+            for load in loads[9:]:
                 load.wait()
         p3 = pressure[None]
         acc = v[...] - jd[:, 0].astype(F32) * p3
@@ -528,7 +565,7 @@
     table = jnp.zeros(hess.shape, F32)
     for i in range(ITERS + 1):
         for j in range(ITERS):
-            table = jnp.where((hr == i) & (hc == j), hessen[i][j], table)
+            table = jnp.where((hr == j) & (hc == i), hessen[i][j], table)
     hess[...] = table
     for condition, wait in finals:
         if condition is None:
@@ -591,27 +628,25 @@
     plane = (length // LANES) * width
     total = depth * plane
     points = depth * width
-    op = level1_op.astype(F32)
-    colsum = jnp.sum(op, axis=0)
-    codiag = jnp.stack([op[a, a] for a in range(aggregates)])
-    lane_pad = ((0, 0), (0, LANES - aggregates))
-    order = (1, 3, 2, 0)
-    colsum = colsum.transpose(order).reshape(total, aggregates)
-    codiag = codiag.transpose(order).reshape(total, aggregates)
-    lvl = jnp.stack(
-        [jnp.pad(colsum, lane_pad), jnp.pad(codiag, lane_pad, constant_values=1.0)]
-    )
+    lvl = level1_op.transpose(0, 2, 3, 4, 1)
     flat = coarsest_inv.shape[2] * coarsest_inv.shape[3]
     co_rows = flat // LANES
-    inv = coarsest_inv.reshape(points * co_rows, LANES)
 
     vm = pl.BlockSpec(memory_space=pltpu.VMEM)
-    sm = pl.BlockSpec(memory_space=pltpu.SMEM)
-    anyspace = pl.BlockSpec(memory_space=pl.ANY)
+    hbm = pl.BlockSpec(memory_space=pltpu.HBM)
     edge_rows = -(-depth // width) * plane
     v = pltpu.VMEM
     dma = pltpu.SemaphoreType.DMA
     scratch = [
+        v((comps, total, LANES), F32),
+        v((comps, total, LANES), jnp.bfloat16),
+        v((total, LANES), jnp.bfloat16),
+        v((6, total, LANES), jnp.bfloat16),
+        v((total, LANES), F32),
+        pltpu.SMEM(well_columns.shape, jnp.int32),
+        v((total, LANES), jnp.int32),
+        v(lvl.shape, jnp.bfloat16),
+        v(coarsest_inv.shape, jnp.bfloat16),
         v((comps, comps, total, LANES), jnp.bfloat16),
         v((6, comps, comps, total, LANES), jnp.bfloat16),
         v((comps, comps, total, LANES), jnp.bfloat16),
@@ -636,7 +671,7 @@
         v((ITERS, count * co_rows, LANES), F32),
         v((5, plane, LANES), F32),
         v((5, layer_devices, plane, LANES), F32),
-        dma((3,)),
+        dma((12,)),
         dma((ROUNDS, 4)), dma((ROUNDS, 4)),
         dma((ITERS, 4)), dma((ITERS, 4)),
         dma((4,)), dma((4,)),
@@ -652,23 +687,23 @@
         out_shape=(
             jax.ShapeDtypeStruct((comps, total, LANES), F32),
             jax.ShapeDtypeStruct((comps, total, LANES), F32),
-            jax.ShapeDtypeStruct((ITERS + 1, ITERS), F32),
+            jax.ShapeDtypeStruct((ITERS, ITERS + 1), F32),
         ),
-        in_specs=[vm, vm, vm, vm, vm, sm, vm, vm, vm, anyspace, anyspace, anyspace],
+        in_specs=[hbm] * 12,
         out_specs=(vm, vm, vm),
         scratch_shapes=scratch,
         compiler_params=pltpu.CompilerParams(
-            collective_id=0, has_side_effects=True, vmem_limit_bytes=40 * 1024 * 1024
+            collective_id=0, has_side_effects=True, vmem_limit_bytes=63 * 1024 * 1024
         ),
     )(
         to_rows(right_side), to_rows(press_weight), to_rows(press_diag), to_rows(press_off),
-        to_rows(well_index), well_columns, to_rows(agg_map), lvl, inv,
+        to_rows(well_index), well_columns, to_rows(agg_map), lvl, coarsest_inv,
         to_rows(jac_diag), to_rows(jac_off), to_rows(block_inv),
     )
     return (
         from_rows(sol, depth, width, length),
         from_rows(res, depth, width, length),
-        hess,
+        hess.T,
     )
 
 

time: 62.7 us -> 52.9 us (0.84)
  local copies, waits for them, and re-layouts: 12.4 us -> 4.26 us
  other arithmetic: 1.56 us -> 0 us
    unnamed x30 -> x3, local copies, waits for them, and re-layouts: 11.3 us -> 4.26 us
    reduce_sum x1 -> x0, other arithmetic: 0.79 us -> none  [on_device(): colsum = jnp.sum(op, axis=0)]
    reshape x1 -> x0, local copies, waits for them, and re-layouts: 0.78 us -> none  [on_device(): inv = coarsest_inv.reshape(points * co_rows, LANES)]
    convert_element_type x1 -> x0, other arithmetic: 0.77 us -> none  [on_device(): op = level1_op.astype(F32)]
where the time goes in v2:
time: 52.9 us; the launch traced here: 52.7 us
  Pallas kernels  47.8 us (90%)
  local copies, waits for them, and re-layouts  4.26 us (8%)
  between operations  0.64 us (1%)
    pallas_call x1, Pallas kernels, on_device(): pl.pallas_call(body, out_shape=(jax.ShapeDtypeStruct((comps, total, LANES...  47.8 us
    unnamed x3, local copies, waits for them, and re-layouts  4.26 us

profile of v2, /device:TPU:0, one launch (start us, length us, event | category | flops | bytes accessed | tf_op | source)
XLA Modules:
  0.0 52.7 jit_solution(17978451314117804895)
XLA Ops:
  0.6 47.8 %shard_map.139 = (f32[12,16,128]{2,1,0:T(8,128)}, f32[12,16,128]{2,1,0:T(8,128)}, f32[2,3]{1,0:T(2,128)}) custom-call(f32[12,16,128]{2,1,0:T(8,128)} %bitcast.62, bf16[12,16,128]{2,1,0:T(8,128)(2,1)} %bitcast.63, bf16[16,128]{1,0:T(8,128)(2,1)} %bitcast.68, bf16[6,16,128]{2,1,0:T(8,128)(2,1)} %bitcast.65, f32[16,128]{1,0:T(8,128)} %bitcast.66, s32[64]{0:T(128)} %wc_hbm.1, ...), custom_call_target="tpu_custom_call" | custom-call | tf_op jit(solution)/shard_map/pallas_call | solution.py:685
  48.5 1.5 %copy.29 = f32[12,2,2,512]{3,2,1,0:T(2,128)} copy(f32[12,2,2,512]{3,2,1,0:T(2,128)} %bitcast.61) | data formatting | bytes 196608
  50.0 1.5 %copy.30 = f32[12,2,2,512]{3,2,1,0:T(2,128)} copy(f32[12,2,2,512]{3,2,1,0:T(2,128)} %bitcast.60) | data formatting | bytes 196608
  51.6 1.2 %copy.31 = f32[3,2]{0,1:T(2,128)} copy(f32[3,2]{0,1:T(2,128)} %bitcast.69) | data formatting | bytes 48

commit v3 on v2

--- a/solution.py
+++ b/solution.py
@@ -452,8 +452,8 @@
         got = halo_read(1 + 3 * t)
         smooth_halos = [got[d] + halo_extra[d][None] for d in range(4)]
         pressure = smooth + (rhs - apply_pressure(smooth, smooth_halos)) / diag
+        well_wait = well_start(1 + 2 * t, pressure)
         halo_d = halo_start(2 + 3 * t, pressure)
-        well_wait = well_start(1 + 2 * t, pressure)
         if t == 0:
             for load in loads[9:]:
                 load.wait()
@@ -483,12 +483,12 @@
         lax.fori_loop(0, comps, correct, 0)
         head = dirs[t, 0] + pressure
         dirs[t, 0] = head
+        well_wait = well_start(2 + 2 * t, head)
         d_all = dirs[t]
         pkx12[t, 0] = pack(d_all, width - 1)
         pkx12[t, 1] = pack(d_all, 0)
         big = big_copies(t)
         start_all(big)
-        well_wait = well_start(2 + 2 * t, head)
         near[4] = shift_yl(d_all)
         near[5] = shift_yh(d_all)
 
@@ -685,15 +685,15 @@
     sol, res, hess = pl.pallas_call(
         body,
         out_shape=(
-            jax.ShapeDtypeStruct((comps, total, LANES), F32),
-            jax.ShapeDtypeStruct((comps, total, LANES), F32),
-            jax.ShapeDtypeStruct((ITERS, ITERS + 1), F32),
+            v((comps, total, LANES), F32),
+            v((comps, total, LANES), F32),
+            v((ITERS, ITERS + 1), F32),
         ),
         in_specs=[hbm] * 12,
         out_specs=(vm, vm, vm),
         scratch_shapes=scratch,
         compiler_params=pltpu.CompilerParams(
-            collective_id=0, has_side_effects=True, vmem_limit_bytes=63 * 1024 * 1024
+            collective_id=0, has_side_effects=True, vmem_limit_bytes=60 * 1024 * 1024
         ),
     )(
         to_rows(right_side), to_rows(press_weight), to_rows(press_diag), to_rows(press_off),

time: 52.9 us -> 49.8 us (0.941)
  local copies, waits for them, and re-layouts: 4.26 us -> 1.84 us
  Pallas kernels: 47.8 us -> 47.2 us
    unnamed x3, local copies, waits for them, and re-layouts: 4.26 us -> 1.84 us
    pallas_call x1, Pallas kernels: 47.8 us -> 47.2 us  [on_device(): pl.pallas_call(body, out_shape=(v((comps, total, LANES), F32), v((comps,...]
where the time goes in v3:
time: 49.8 us; the launch traced here: 49.7 us
  Pallas kernels  47.2 us (95%)
  local copies, waits for them, and re-layouts  1.84 us (4%)
  between operations  0.64 us (1%)
    pallas_call x1, Pallas kernels, on_device(): pl.pallas_call(body, out_shape=(v((comps, total, LANES), F32), v((comps,...  47.2 us
    unnamed x3, local copies, waits for them, and re-layouts  1.84 us

profile of v3, /device:TPU:0, one launch (start us, length us, event | category | flops | bytes accessed | tf_op | source)
XLA Modules:
  0.0 49.7 jit_solution(545665619981409026)
XLA Ops:
  0.6 47.2 %shard_map.139 = (f32[12,16,128]{2,1,0:T(8,128)S(1)}, f32[12,16,128]{2,1,0:T(8,128)S(1)}, f32[2,3]{1,0:T(2,128)S(1)}) custom-call(f32[12,16,128]{2,1,0:T(8,128)} %bitcast.63, bf16[12,16,128]{2,1,0:T(8,128)(2,1)} %bitcast.64, bf16[16,128]{1,0:T(8,128)(2,1)} %bitcast.69, bf16[6,16,128]{2,1,0:T(8,128)(2,1)} %bitcast.66, f32[16,128]{1,0:T(8,128)} %bitcast.67, ...), custom_call_target="tpu_custom_call" | custom-call | tf_op jit(solution)/shard_map/pallas_call | solution.py:685
  47.8 0.6 %copy.29 = f32[12,2,2,512]{3,2,1,0:T(2,128)} copy(f32[12,2,2,512]{3,2,1,0:T(2,128)S(1)} %bitcast.58) | data formatting | bytes 196608
  48.5 0.6 %copy.30 = f32[12,2,2,512]{3,2,1,0:T(2,128)} copy(f32[12,2,2,512]{3,2,1,0:T(2,128)S(1)} %bitcast.57) | data formatting | bytes 196608
  49.1 0.6 %copy.31 = f32[3,2]{0,1:T(2,128)} copy(f32[3,2]{0,1:T(2,128)S(1)} %bitcast.59) | data formatting | bytes 48
